TPU v7x, 128 devices: a whole 4x4x4 slice. The times are simulated.
128 devices in a mesh: rows: 2 (over core), cols: 64 (over z, y, x).
Axes of the slice: x: 4, y: 4, z: 4, core: 2. Of those that a mesh axis runs over, the one named last changes fastest.
Arguments:
- row_geom: float32 [3072, 8, 1024], P('cols', None, 'rows'), may hold values from -1 to 1
- col_geom: float32 [3072, 8, 1024], P('cols', None, 'rows'), may hold values from -1 to 1
- row_start: int32 [3072], P('cols'), may hold values from 1024 to 397951
- col_start: int32 [3072], P('cols'), may hold values from 512 to 398463, as said below
- block_count: int32 [64], P('cols'), may hold values from 1 to 48, 768 in all
- sketch: float32 [1024, 64], replicated, may hold values from -0.75 to 0.75
Outputs:
- left_factor: float32 [3072, 64, 1024], P('cols', None, 'rows')
- right_factor: float32 [3072, 64, 1024], P('cols', None, 'rows')
Inputs may be any that keep to these rules, and one draw needn't show every extreme that they name: `block_count`: each owner's counts are at most 48; all counts together sum to exactly 48 // 4 times the number of owners. Places beyond an owner's count are unused. col_start minus row_start lies between -512 and 512.
All inputs are finite; a program needn't handle non-finite values. No bound on the sum of `block_count` on one device may be relied on, other than what follows from the above.
Results may differ from a plain program's by a relative error of at most 0.0003.
Values sent between devices are 32-bit elements; how exact they have to be, the bound alone decides.
A program may use at most 128 MiB of HBM per device.

v0:
```python
import jax
import jax.numpy as jnp
from jax import lax
from jax.sharding import PartitionSpec as P

HIGHEST = lax.Precision.HIGHEST


def copy_for_each(shard, axis):
    copies = jnp.broadcast_to(shard, (lax.axis_size(axis), *shard.shape))
    return lax.all_to_all(copies, axis, split_axis=0, concat_axis=0, tiled=True)


def combined_pairwise(pieces, combine):
    while len(jax.tree.leaves(pieces)[0]) > 1:
        pieces = jax.vmap(combine)(*(pieces[side::2] for side in (0, 1)))
    return pieces[0]


def carried_in(shard, axis, combine, identity):
    count, here = (lax.axis_size(axis), lax.axis_index(axis))
    passed = jnp.arange(count) < here

    def kept(part, zero, own):
        part = jnp.where(
            passed.reshape(-1, *(1 for _ in own.shape)), part, jnp.asarray(zero, own.dtype)
        )
        return part

    pieces = copy_for_each(shard, axis)
    return combined_pairwise(kept(pieces, identity, shard), combine)


def kernel_block(row_geo, col_geo, start_row, start_col):
    sep_x = row_geo[:, 0, :, None] - col_geo[:, 0, None, :]
    sep_y = row_geo[:, 1, :, None] - col_geo[:, 1, None, :]
    sep_z = row_geo[:, 2, :, None] - col_geo[:, 2, None, :]
    row_area = 0.1 + 0.05 * row_geo[:, 6, :, None]
    col_area = 0.1 + 0.05 * col_geo[:, 6, None, :]
    inverse = 1.0 / (sep_x * sep_x + sep_y * sep_y + sep_z * sep_z + row_area + col_area)
    normal_dot = (
        row_geo[:, 3, :, None] * col_geo[:, 3, None, :]
        + row_geo[:, 4, :, None] * col_geo[:, 4, None, :]
        + row_geo[:, 5, :, None] * col_geo[:, 5, None, :]
    )
    row_proj = (
        row_geo[:, 3, :, None] * sep_x
        + row_geo[:, 4, :, None] * sep_y
        + row_geo[:, 5, :, None] * sep_z
    )
    col_proj = (
        col_geo[:, 3, None, :] * sep_x
        + col_geo[:, 4, None, :] * sep_y
        + col_geo[:, 5, None, :] * sep_z
    )
    influence = (
        col_area * (normal_dot - 3.0 * row_proj * col_proj * inverse) * inverse * jnp.sqrt(inverse)
    )
    self_term = 4.0 + 2.0 * row_geo[:, 7, :, None]
    row_ids = jnp.arange(row_geo.shape[2], dtype=jnp.int32)[:, None]
    col_ids = jnp.arange(col_geo.shape[2], dtype=jnp.int32)[None, :]
    distance = (start_row - start_col)[:, None, None]
    match = (col_ids - row_ids)[None, :, :] == distance
    return jnp.where(match, self_term, influence)


def factor_pair(gram, projected):
    rank = gram.shape[1]
    trace = jnp.trace(gram, axis1=1, axis2=2)
    ridge = 0.01 * trace / rank + 0.001
    system = gram + ridge[:, None, None] * jnp.eye(rank, dtype=gram.dtype)[None]
    lower = jnp.linalg.cholesky(system)
    half = lax.linalg.triangular_solve(lower, projected, left_side=True, lower=True)
    return lax.linalg.triangular_solve(lower, half, left_side=True, lower=True, transpose_a=True)


def pick_group(total, most):
    group = most
    while total % group:
        group -= 1
    return group


def add_counts(earlier, later):
    return earlier + later


def whole_compress(row_geo, col_geo, row_start, col_start, sketch):
    slots, geo_count, width = row_geo.shape
    rank = sketch.shape[1]
    ranks = lax.axis_size("rows")
    my_index = lax.axis_index("rows")
    turns = slots // ranks
    stacked = jnp.stack([row_geo, col_geo], 1).reshape(turns, ranks, 2, geo_count, width)
    gathered = lax.all_to_all(stacked, "rows", split_axis=1, concat_axis=4, tiled=True)
    full_width = gathered.shape[4]
    full_rows = gathered[:, 0, 0]
    full_cols = gathered[:, 0, 1]
    my_row_start = lax.dynamic_index_in_dim(
        row_start.reshape(turns, ranks), my_index, 1, keepdims=False
    )
    my_col_start = lax.dynamic_index_in_dim(
        col_start.reshape(turns, ranks), my_index, 1, keepdims=False
    )
    group = pick_group(turns, 2)
    batches = turns // group

    def step(carry, packed):
        rows_part, cols_part, first_row, first_col = packed
        block = kernel_block(rows_part, cols_part, first_row, first_col)
        sketched = jnp.einsum("gik,kr->gir", block, sketch, precision=HIGHEST)
        gram = jnp.einsum("gir,gis->grs", sketched, sketched, precision=HIGHEST)
        projected = jnp.einsum("gik,gir->grk", block, sketched, precision=HIGHEST)
        right = factor_pair(gram, projected)
        left = jnp.transpose(sketched, (0, 2, 1))
        return (carry, jnp.stack([left, right], 1))

    packed = (
        full_rows.reshape(batches, group, geo_count, full_width),
        full_cols.reshape(batches, group, geo_count, full_width),
        my_row_start.reshape(batches, group),
        my_col_start.reshape(batches, group),
    )
    results = lax.scan(step, jnp.int32(0), packed)[1]
    results = results.reshape(turns, 1, 2, rank, full_width)
    returned = lax.all_to_all(results, "rows", split_axis=4, concat_axis=1, tiled=True)
    flat = returned.reshape(slots, 2, rank, width)
    return (flat[:, 0], flat[:, 1])


def compress(row_geo, col_geo, row_start, col_start, sketch):
    return whole_compress(row_geo, col_geo, row_start, col_start, sketch)


def on_device(row_geom, col_geom, row_start, col_start, block_count, sketch):
    owned, geo_count, width = row_geom.shape
    rank = sketch.shape[1]
    count = block_count[0]
    order = jnp.arange(owned, dtype=jnp.int32)
    owners = lax.axis_size("cols")
    capacity = -(-owned // owners)
    total_slots = owners * capacity
    start = carried_in(count, "cols", add_counts, jnp.int32(0))
    workers = jnp.arange(owners, dtype=jnp.int32)[:, None]
    places = jnp.arange(capacity, dtype=jnp.int32)[None, :]
    picked = places * owners + (workers - start) % owners
    is_sent = picked < count
    safe = jnp.minimum(picked, owned - 1)
    send_rows = jnp.where(is_sent[:, :, None, None], row_geom[safe], 0.0)
    send_cols = jnp.where(is_sent[:, :, None, None], col_geom[safe], 0.0)
    send_ranges = jnp.stack(
        [
            jnp.where(is_sent, row_start[safe], 0),
            jnp.where(is_sent, col_start[safe], 0),
            jnp.where(is_sent, start + picked, -1),
        ],
        2,
    ).astype(jnp.float32)
    got_rows, got_cols, got_ranges = (
        lax.all_to_all(send_rows, "cols", split_axis=0, concat_axis=0, tiled=True),
        lax.all_to_all(send_cols, "cols", split_axis=0, concat_axis=0, tiled=True),
        lax.all_to_all(send_ranges, "cols", split_axis=0, concat_axis=0, tiled=True),
    )
    ranges = got_ranges.reshape(total_slots, 3).astype(jnp.int32)
    busy = owned // 4
    flat_ids = ranges[:, 2]
    is_live = flat_ids >= 0
    target = jnp.where(is_live, flat_ids // owners, busy)
    chosen = target[None, :] == jnp.arange(busy, dtype=jnp.int32)[:, None]
    source = jnp.sum(
        jnp.where(chosen, jnp.arange(total_slots, dtype=jnp.int32)[None, :], 0), axis=1
    )
    busy_rows = got_rows.reshape(total_slots, geo_count, width)[source]
    busy_cols = got_cols.reshape(total_slots, geo_count, width)[source]
    left_busy, right_busy = compress(
        busy_rows, busy_cols, ranges[source, 0], ranges[source, 1], sketch
    )
    slot_pick = jnp.minimum(target, busy - 1)
    back_left = jnp.where(is_live[:, None, None], left_busy[slot_pick], 0.0).reshape(
        owners, capacity, rank, width
    )
    back_right = jnp.where(is_live[:, None, None], right_busy[slot_pick], 0.0).reshape(
        owners, capacity, rank, width
    )
    returned_left, returned_right = (
        lax.all_to_all(back_left, "cols", split_axis=0, concat_axis=0, tiled=True),
        lax.all_to_all(back_right, "cols", split_axis=0, concat_axis=0, tiled=True),
    )
    flat_index = (start + order) % owners * capacity + order // owners
    left = returned_left.reshape(total_slots, rank, width)[flat_index]
    right = returned_right.reshape(total_slots, rank, width)[flat_index]
    is_kept = (order < count)[:, None, None]
    return (jnp.where(is_kept, left, 0.0), jnp.where(is_kept, right, 0.0))


def solution(mesh):
    placed = (
        P("cols", None, "rows"),
        P("cols", None, "rows"),
        P("cols"),
        P("cols"),
        P("cols"),
        P(),
    )
    return jax.shard_map(
        on_device,
        mesh=mesh,
        in_specs=placed,
        out_specs=(P("cols", None, "rows"), P("cols", None, "rows")),
        check_vma=False,
    )
```

profile of v0, /device:TPU:4, one launch (start us, length us, event | category | flops | bytes accessed | tf_op | source)
XLA Modules:
  0.0 634.6 jit_solution(12272790962720469400)
XLA Ops:
  2.0 11.5 %all-to-all-start = ((s32[64,1,1]{2,1,0:T(1,128)}), s32[64,1,1]{2,1,0:T(1,128)S(1)}, u32[]{:S(2)}, u32[]{:S(2)}) async-start(s32[64,1,1]{2,1,0:T(1,128)} %broadcast_in_dim.145), calls=%async_computation | async-start | bytes 65536 | tf_op jit(solution)/shard_map/all_to_all | solution.py:11
  45.2 20.9 %all_to_all.67 = f32[64,1,8,512]{3,2,1,0:T(8,128)S(1)} all-to-all(f32[64,1,8,512]{3,2,1,0:T(8,128)S(1)} %get-tuple-element.163), channel_id=1, replica_groups=mesh['rows'=2,'cols'=64] {'cols'}, dimensions={0} | all-to-all | bytes 2097152 | tf_op jit(solution)/shard_map/all_to_all | solution.py:160
  75.9 10.3 %all-to-all-done.3 = f32[64,1,8,512]{3,2,1,0:T(8,128)S(1)} async-done(((f32[64,1,8,512]{3,2,1,0:T(8,128)}), f32[64,1,8,512]{3,2,1,0:T(8,128)S(1)}, u32[]{:S(2)}, u32[]{:S(2)}) %all-to-all-start.3) | async-done | bytes 1048608 | tf_op jit(solution)/shard_map/all_to_all | solution.py:161
  90.9 208.2 %while.12 = (s32[]{:T(128)}, f32[3,2,2,64,1024]{4,3,2,1,0:T(8,128)}, s32[3,2]{1,0:T(4,128)S(1)}, s32[3,2]{1,0:T(4,128)S(1)}, f32[3,2,8,1024]{3,2,1,0:T(8,128)S(1...) while((s32[]{:T(128)}, f32[3,2,2,64,1024]{4,3,2,1,0:T(8,128)}, ...), condition=%wide.region_5.6_spmd, body=%wide.region_1.5_spmd.sunk | while | flops 3671470336 | bytes 37377732 | solution.py:124
  92.0 21.5 %fusion.96 = f32[2,1024,64]{1,2,0:T(8,128)S(1)} fusion(f32[2,1024]{1,0:T(2,128)S(1)} %get-tuple-element.239, f32[2,1024]{1,0:T(2,128)S(1)} %get-tuple-element.241, f32[2,1024]{1,0:T(2,128)S(1)} %get-tuple-element.242, f32[2,1024]{1,0:T(2,128)S(1)} %get-tuple-element.243, f32[2,1024]{1,0:T(2,128)S(1)} %get-tuple-element.244, ...), kind=kOutput, calls=%fused_computation.40.clone.1 | convolution fusion | flops 1684013056 | bytes 5103624 | tf_op jit(solution)/shard_map/while/body/eval_jaxpr/gik,kr->gir/dot_general | solution.py:111
  114.4 11.7 %custom-call.42 = f32[2,64,64]{2,1,0:T(8,128)S(1)} custom-call(f32[2,64,64]{2,1,0:T(8,128)S(1)} %fusion.99), custom_call_target="Cholesky" | custom-call | tf_op jit(solution)/shard_map/while/body/eval_jaxpr/jit(cholesky)/cholesky | solution.py:72
  126.4 10.0 %custom-call.43 = f32[2,1,64,64]{2,3,1,0:T(8,128)S(1)} custom-call(f32[2,1,64,64]{3,2,1,0:T(8,128)S(1)} %select_bitcast_fusion.3), custom_call_target="InvertDiagBlocksLowerTriangular" | custom-call | tf_op jit(solution)/shard_map/while/body/eval_jaxpr/triangular_solve | solution.py:74
  136.4 20.7 %fusion.97 = f32[2,64,1024]{2,1,0:T(8,128)S(1)} fusion(f32[2,1024,64]{1,2,0:T(8,128)S(1)} %fusion.96, f32[2,1024]{1,0:T(2,128)S(1)} %get-tuple-element.239, f32[2,1024]{1,0:T(2,128)S(1)} %get-tuple-element.241, f32[2,1024]{1,0:T(2,128)S(1)} %get-tuple-element.242, f32[2,1024]{1,0:T(2,128)S(1)} %get-tuple-element.243, ...), kind=kOutput, calls=%fused_computation.39.clone.1 | convolution fusion | flops 1684013056 | bytes 5365768 | tf_op jit(solution)/shard_map/while/body/eval_jaxpr/gik,gir->grk/dot_general | solution.py:113
  160.5 21.1 %fusion.96 = f32[2,1024,64]{1,2,0:T(8,128)S(1)} fusion(f32[2,1024]{1,0:T(2,128)S(1)} %get-tuple-element.239, f32[2,1024]{1,0:T(2,128)S(1)} %get-tuple-element.241, f32[2,1024]{1,0:T(2,128)S(1)} %get-tuple-element.242, f32[2,1024]{1,0:T(2,128)S(1)} %get-tuple-element.243, f32[2,1024]{1,0:T(2,128)S(1)} %get-tuple-element.244, ...), kind=kOutput, calls=%fused_computation.40.clone.1 | convolution fusion | flops 1684013056 | bytes 5103624 | tf_op jit(solution)/shard_map/while/body/eval_jaxpr/gik,kr->gir/dot_general | solution.py:111
  182.5 11.7 %custom-call.42 = f32[2,64,64]{2,1,0:T(8,128)S(1)} custom-call(f32[2,64,64]{2,1,0:T(8,128)S(1)} %fusion.99), custom_call_target="Cholesky" | custom-call | tf_op jit(solution)/shard_map/while/body/eval_jaxpr/jit(cholesky)/cholesky | solution.py:72
  194.5 10.0 %custom-call.43 = f32[2,1,64,64]{2,3,1,0:T(8,128)S(1)} custom-call(f32[2,1,64,64]{3,2,1,0:T(8,128)S(1)} %select_bitcast_fusion.3), custom_call_target="InvertDiagBlocksLowerTriangular" | custom-call | tf_op jit(solution)/shard_map/while/body/eval_jaxpr/triangular_solve | solution.py:74
  204.6 20.8 %fusion.97 = f32[2,64,1024]{2,1,0:T(8,128)S(1)} fusion(f32[2,1024,64]{1,2,0:T(8,128)S(1)} %fusion.96, f32[2,1024]{1,0:T(2,128)S(1)} %get-tuple-element.239, f32[2,1024]{1,0:T(2,128)S(1)} %get-tuple-element.241, f32[2,1024]{1,0:T(2,128)S(1)} %get-tuple-element.242, f32[2,1024]{1,0:T(2,128)S(1)} %get-tuple-element.243, ...), kind=kOutput, calls=%fused_computation.39.clone.1 | convolution fusion | flops 1684013056 | bytes 5365768 | tf_op jit(solution)/shard_map/while/body/eval_jaxpr/gik,gir->grk/dot_general | solution.py:113
  228.6 21.1 %fusion.96 = f32[2,1024,64]{1,2,0:T(8,128)S(1)} fusion(f32[2,1024]{1,0:T(2,128)S(1)} %get-tuple-element.239, f32[2,1024]{1,0:T(2,128)S(1)} %get-tuple-element.241, f32[2,1024]{1,0:T(2,128)S(1)} %get-tuple-element.242, f32[2,1024]{1,0:T(2,128)S(1)} %get-tuple-element.243, f32[2,1024]{1,0:T(2,128)S(1)} %get-tuple-element.244, ...), kind=kOutput, calls=%fused_computation.40.clone.1 | convolution fusion | flops 1684013056 | bytes 5103624 | tf_op jit(solution)/shard_map/while/body/eval_jaxpr/gik,kr->gir/dot_general | solution.py:111
  250.7 11.7 %custom-call.42 = f32[2,64,64]{2,1,0:T(8,128)S(1)} custom-call(f32[2,64,64]{2,1,0:T(8,128)S(1)} %fusion.99), custom_call_target="Cholesky" | custom-call | tf_op jit(solution)/shard_map/while/body/eval_jaxpr/jit(cholesky)/cholesky | solution.py:72
  262.7 10.2 %custom-call.43 = f32[2,1,64,64]{2,3,1,0:T(8,128)S(1)} custom-call(f32[2,1,64,64]{3,2,1,0:T(8,128)S(1)} %select_bitcast_fusion.3), custom_call_target="InvertDiagBlocksLowerTriangular" | custom-call | tf_op jit(solution)/shard_map/while/body/eval_jaxpr/triangular_solve | solution.py:74
  272.9 20.6 %fusion.97 = f32[2,64,1024]{2,1,0:T(8,128)S(1)} fusion(f32[2,1024,64]{1,2,0:T(8,128)S(1)} %fusion.96, f32[2,1024]{1,0:T(2,128)S(1)} %get-tuple-element.239, f32[2,1024]{1,0:T(2,128)S(1)} %get-tuple-element.241, f32[2,1024]{1,0:T(2,128)S(1)} %get-tuple-element.242, f32[2,1024]{1,0:T(2,128)S(1)} %get-tuple-element.243, ...), kind=kOutput, calls=%fused_computation.39.clone.1 | convolution fusion | flops 1684013056 | bytes 5365768 | tf_op jit(solution)/shard_map/while/body/eval_jaxpr/gik,gir->grk/dot_general | solution.py:113
  308.5 9.6 %reshape.618 = f32[2,1,393216]{2,1,0:T(1,128)} reshape(f32[1024,1,6,2,64]{4,3,2,1,0:T(2,128)} %bitcast.201) | data formatting | bytes 6291456
  318.1 10.8 %all_to_all.69 = f32[2,1,393216]{2,1,0:T(1,128)} all-to-all(f32[2,1,393216]{2,1,0:T(1,128)} %reshape.618), channel_id=1, replica_groups=mesh['rows'=2,'cols'=64] {'rows'}, dimensions={0} | all-to-all | bytes 6291456 | tf_op jit(solution)/shard_map/all_to_all | solution.py:126
  329.4 12.6 %reduce.17 = f32[2,393216]{1,0:T(2,128)} reduce(f32[2,1,393216]{2,1,0:T(1,128)} %all_to_all.69, f32[]{:T(128)} %broadcast.1032), dimensions={1}, to_apply=%all_to_all.54.reduce_sub_computation | reduce | bytes 6291460 | tf_op jit(solution)/shard_map/all_to_all | solution.py:126
  342.0 10.4 %reshape.619 = f32[1024,1,6,2,64]{4,3,2,1,0:T(2,128)} reshape(f32[2,393216]{1,0:T(2,128)} %reduce.17) | data formatting | bytes 6291456
  376.1 9.4 %fusion.41 = (f32[64,1,64,512]{3,2,1,0:T(8,128)}, f32[64,1,64,512]{3,2,1,0:T(8,128)S(1)}) fusion(f32[64,64,512]{2,1,0:T(8,128)} %gather_fusion.10, pred[64]{0:T(512)(128)(4,1)S(1)} %copy-done.3, f32[64,64,512]{2,1,0:T(8,128)} %gather_fusion.8), kind=kLoop, calls=%fused_computation.95 | loop fusion | flops 4194304 | bytes 33554496 | tf_op jit(solution)/shard_map/jit(_where)/select_n | solution.py:182
  385.5 102.9 %all_to_all.70 = f32[64,1,64,512]{3,2,1,0:T(8,128)} all-to-all(f32[64,1,64,512]{3,2,1,0:T(8,128)S(1)} %get-tuple-element.162), channel_id=1, replica_groups=mesh['rows'=2,'cols'=64] {'cols'}, dimensions={0} | all-to-all | bytes 16777216 | tf_op jit(solution)/shard_map/all_to_all | solution.py:186
  503.4 111.5 %all-to-all-done.7 = f32[64,1,64,512]{3,2,1,0:T(8,128)} async-done(((f32[64,1,64,512]{3,2,1,0:T(8,128)}), f32[64,1,64,512]{3,2,1,0:T(8,128)}, u32[]{:S(2)}, u32[]{:S(2)}) %all-to-all-start.7) | async-done | bytes 8388640 | tf_op jit(solution)/shard_map/all_to_all | solution.py:187
  622.0 12.4 %broadcast_select_fusion = (f32[48,64,512]{2,1,0:T(8,128)}, f32[48,64,512]{2,1,0:T(8,128)}) fusion(f32[48,64,512]{2,1,0:T(8,128)} %gather_fusion.11, pred[48]{0:T(512)(128)(4,1)S(1)} %iota_compare_fusion.4, f32[48,64,512]{2,1,0:T(8,128)} %gather_fusion.9), kind=kLoop, calls=%fused_computation.98 | loop fusion | flops 3145728 | bytes 25165872 | tf_op jit(solution)/shard_map/jit(_where)/select_n | solution.py:193
  (146 shorter events, 113.5 us)
Async XLA Ops:
  0.6 35.2 %copy-start = (f32[48,8,512]{2,1,0:T(8,128)S(1)}, f32[48,8,512]{2,1,0:T(8,128)}, u32[]{:S(2)}) copy-start(f32[48,8,512]{2,1,0:T(8,128)} %param.8) | copy-start | bytes 2359300
  2.0 19.0 %all-to-all-start = ((s32[64,1,1]{2,1,0:T(1,128)}), s32[64,1,1]{2,1,0:T(1,128)S(1)}, u32[]{:S(2)}, u32[]{:S(2)}) async-start(s32[64,1,1]{2,1,0:T(1,128)} %broadcast_in_dim.145), calls=%async_computation | async-start | bytes 65536 | tf_op jit(solution)/shard_map/all_to_all | solution.py:11
  28.9 14.4 %all-to-all-start.1 = ((f32[64,1,3]{2,1,0:T(1,128)}), f32[64,1,3]{2,1,0:T(1,128)S(1)}, u32[]{:S(2)}, u32[]{:S(2)}) async-start(f32[64,1,3]{2,1,0:T(1,128)} %copy.46), calls=%async_computation.1 | async-start | bytes 65536 | tf_op jit(solution)/shard_map/all_to_all | solution.py:162
  36.5 54.5 %copy-start.4 = (f32[1024,64]{0,1:T(8,128)S(1)}, f32[1024,64]{0,1:T(8,128)}, u32[]{:S(2)}) copy-start(f32[1024,64]{0,1:T(8,128)} %param.13) | copy-start | bytes 786436
  66.1 20.0 %all-to-all-start.3 = ((f32[64,1,8,512]{3,2,1,0:T(8,128)}), f32[64,1,8,512]{3,2,1,0:T(8,128)S(1)}, u32[]{:S(2)}, u32[]{:S(2)}) async-start(f32[64,1,8,512]{3,2,1,0:T(8,128)} %get-tuple-element.164), calls=%async_computation.3 | async-start | bytes 2097152 | tf_op jit(solution)/shard_map/all_to_all | solution.py:161
  92.0 21.5 %copy-start.2 = (s32[1024,1024]{1,0:T(8,128)}, s32[1024,1024]{1,0:T(8,128)S(1)}, u32[]{:S(2)}) copy-start(s32[1024,1024]{1,0:T(8,128)S(1)} %iota_subtract_fusion.2) | copy-start | bytes 12582916 | tf_op jit(solution)/shard_map/while
  160.5 21.1 %copy-start.2 = (s32[1024,1024]{1,0:T(8,128)}, s32[1024,1024]{1,0:T(8,128)S(1)}, u32[]{:S(2)}) copy-start(s32[1024,1024]{1,0:T(8,128)S(1)} %iota_subtract_fusion.2) | copy-start | bytes 12582916 | tf_op jit(solution)/shard_map/while
  228.6 21.2 %copy-start.2 = (s32[1024,1024]{1,0:T(8,128)}, s32[1024,1024]{1,0:T(8,128)S(1)}, u32[]{:S(2)}) copy-start(s32[1024,1024]{1,0:T(8,128)S(1)} %iota_subtract_fusion.2) | copy-start | bytes 12582916 | tf_op jit(solution)/shard_map/while
  371.5 4.6 copy-start.3
  488.4 126.5 %all-to-all-start.7 = ((f32[64,1,64,512]{3,2,1,0:T(8,128)}), f32[64,1,64,512]{3,2,1,0:T(8,128)}, u32[]{:S(2)}, u32[]{:S(2)}) async-start(f32[64,1,64,512]{3,2,1,0:T(8,128)} %get-tuple-element.161), calls=%async_computation.7 | async-start | bytes 16777216 | tf_op jit(solution)/shard_map/all_to_all | solution.py:187
  614.9 19.5 %copy-start.1 = (f32[48,8,512]{2,1,0:T(8,128)S(1)}, f32[48,8,512]{2,1,0:T(8,128)}, u32[]{:S(2)}) copy-start(f32[48,8,512]{2,1,0:T(8,128)} %param.8) | copy-start | bytes 2359300
where the time goes:
time: 641 us; the launch traced here: 635 us
  blocking collectives  139 us (22%)
  waiting for transfers between devices  134 us (21%)
  matrix products  131 us (20%)
  other arithmetic  110 us (17%)
  local copies, waits for them, and re-layouts  80 us (12%)
  starting transfers between devices  32.7 us (5%)
    all_to_all x1, waiting for transfers between devices, on_device(): lax.all_to_all(back_right, 'cols', split_axis=0, concat_axis=0, tiled=True)  112 us
    all_to_all x1, blocking collectives, on_device(): lax.all_to_all(back_left, 'cols', split_axis=0, concat_axis=0, tiled=True)  103 us
    dot_general x3, matrix products, step(): sketched = jnp.einsum('gik,kr->gir', block, sketch, precision=HIGHEST)  63.7 us
    dot_general x3, matrix products, step(): projected = jnp.einsum('gik,gir->grk', block, sketched, precision=HIGHEST)  62.1 us
    another operation x12, other arithmetic, factor_pair(): lower = jnp.linalg.cholesky(system)  35.7 us
    another operation x9, other arithmetic, factor_pair(): lax.linalg.triangular_solve(lower, half, left_side=True, lower=True, tran...  30.5 us
    all_to_all x1, blocking collectives, on_device(): lax.all_to_all(send_rows, 'cols', split_axis=0, concat_axis=0, tiled=True)  20.9 us
    unnamed x10, local copies, waits for them, and re-layouts  20 us
  transfers between devices with their start and end apart: 4, of which 4 were waited for; matrix products, arithmetic and copies ran while one was open for 2% of the time, Pallas kernels for 0%

commit v1 on v0

--- a/solution.py
+++ b/solution.py
@@ -1,9 +1,22 @@
+import functools
 import jax
 import jax.numpy as jnp
 from jax import lax
 from jax.sharding import PartitionSpec as P
 
 HIGHEST = lax.Precision.HIGHEST
+
+
+def press_the_surface(state, lane_axis, array_dim, dim_at):
+    return jnp.concatenate(
+        lax.all_to_all(
+            jnp.stack(jnp.split(state, lax.psum(1, lane_axis), axis=array_dim)), lane_axis, 0, 0
+        ),
+        axis=dim_at,
+    )
+
+
+switch_outputs = functools.partial(press_the_surface, lane_axis="rows", array_dim=4, dim_at=1)
 
 
 def copy_for_each(shard, axis):
@@ -123,7 +136,7 @@
     )
     results = lax.scan(step, jnp.int32(0), packed)[1]
     results = results.reshape(turns, 1, 2, rank, full_width)
-    returned = lax.all_to_all(results, "rows", split_axis=4, concat_axis=1, tiled=True)
+    returned = switch_outputs(results)
     flat = returned.reshape(slots, 2, rank, width)
     return (flat[:, 0], flat[:, 1])
 

time: 641 us -> 588 us (0.917)
  local copies, waits for them, and re-layouts: 80 us -> 40.9 us
  other arithmetic: 110 us -> 97.6 us
    unnamed x10 -> x8, local copies, waits for them, and re-layouts: 20 us -> 0.03 us
    all_to_all x1 -> x0, other arithmetic: 12.6 us -> none  [whole_compress(): lax.all_to_all(results, 'rows', split_axis=4, concat_axis=1, tiled=True)]
    all_to_all x3 -> x0, local copies, waits for them, and re-layouts: 12.4 us -> none  [whole_compress(): lax.all_to_all(results, 'rows', split_axis=4, concat_axis=1, tiled=True)]
    reshape x1, local copies, waits for them, and re-layouts: 9.42 us -> 0.46 us  [press_the_surface(): jnp.concatenate(lax.all_to_all(jnp.stack(jnp.split(state, lax.psum(1, lan...]
where the time goes in v1:
time: 588 us; the launch traced here: 582 us
  waiting for transfers between devices  134 us (23%)
  blocking collectives  134 us (23%)
  matrix products  131 us (22%)
  other arithmetic  97.6 us (17%)
  local copies, waits for them, and re-layouts  40.9 us (7%)
  starting transfers between devices  32.7 us (6%)
  loops' own time  7.75 us (1%)
    all_to_all x1, waiting for transfers between devices, on_device(): lax.all_to_all(back_right, 'cols', split_axis=0, concat_axis=0, tiled=True)  112 us
    all_to_all x1, blocking collectives, on_device(): lax.all_to_all(back_left, 'cols', split_axis=0, concat_axis=0, tiled=True)  103 us
    dot_general x3, matrix products, step(): sketched = jnp.einsum('gik,kr->gir', block, sketch, precision=HIGHEST)  63.6 us
    dot_general x3, matrix products, step(): projected = jnp.einsum('gik,gir->grk', block, sketched, precision=HIGHEST)  62.1 us
    another operation x12, other arithmetic, factor_pair(): lower = jnp.linalg.cholesky(system)  35.7 us
    another operation x9, other arithmetic, factor_pair(): lax.linalg.triangular_solve(lower, half, left_side=True, lower=True, tran...  30.5 us
    all_to_all x1, blocking collectives, on_device(): lax.all_to_all(send_rows, 'cols', split_axis=0, concat_axis=0, tiled=True)  20.9 us
    select_n x1, other arithmetic, on_device(): return (jnp.where(is_kept, left, 0.0), jnp.where(is_kept, right, 0.0))  12.4 us
  transfers between devices with their start and end apart: 4, of which 4 were waited for; matrix products, arithmetic and copies ran while one was open for 2% of the time, Pallas kernels for 0%

profile of v1, /device:TPU:4, one launch (start us, length us, event | category | flops | bytes accessed | tf_op | source)
XLA Modules:
  0.0 582.0 jit_solution(8813023206905552363)
XLA Ops:
  2.0 11.5 %all-to-all-start = ((s32[64,1,1]{2,1,0:T(1,128)}), s32[64,1,1]{2,1,0:T(1,128)S(1)}, u32[]{:S(2)}, u32[]{:S(2)}) async-start(s32[64,1,1]{2,1,0:T(1,128)} %broadcast_in_dim.145), calls=%async_computation | async-start | bytes 65536 | tf_op jit(solution)/shard_map/all_to_all | solution.py:24
  13.5 7.5 %all-to-all-done = s32[64,1,1]{2,1,0:T(1,128)S(1)} async-done(((s32[64,1,1]{2,1,0:T(1,128)}), s32[64,1,1]{2,1,0:T(1,128)S(1)}, u32[]{:S(2)}, u32[]{:S(2)}) %all-to-all-start) | async-done | bytes 288 | tf_op jit(solution)/shard_map/all_to_all | solution.py:24
  45.2 20.9 %all_to_all.57 = f32[64,1,8,512]{3,2,1,0:T(8,128)S(1)} all-to-all(f32[64,1,8,512]{3,2,1,0:T(8,128)S(1)} %get-tuple-element.165), channel_id=1, replica_groups=mesh['rows'=2,'cols'=64] {'cols'}, dimensions={0} | all-to-all | bytes 2097152 | tf_op jit(solution)/shard_map/all_to_all | solution.py:173
  75.9 10.3 %all-to-all-done.3 = f32[64,1,8,512]{3,2,1,0:T(8,128)S(1)} async-done(((f32[64,1,8,512]{3,2,1,0:T(8,128)}), f32[64,1,8,512]{3,2,1,0:T(8,128)S(1)}, u32[]{:S(2)}, u32[]{:S(2)}) %all-to-all-start.3) | async-done | bytes 1048608 | tf_op jit(solution)/shard_map/all_to_all | solution.py:174
  90.9 211.2 %while.12 = (s32[]{:T(128)}, f32[3,2,2,64,1024]{4,3,2,1,0:T(8,128)}, s32[3,2]{1,0:T(4,128)S(1)}, s32[3,2]{1,0:T(4,128)S(1)}, f32[3,2,8,1024]{3,2,1,0:T(8,128)S(1...) while((s32[]{:T(128)}, f32[3,2,2,64,1024]{4,3,2,1,0:T(8,128)}, ...), condition=%wide.region_5.6_spmd, body=%wide.region_1.5_spmd.sunk | while | flops 3671470336 | bytes 37377732 | solution.py:137
  92.1 21.3 %fusion.96 = f32[2,1024,64]{1,2,0:T(8,128)S(1)} fusion(f32[2,1024]{1,0:T(2,128)S(1)} %get-tuple-element.241, f32[2,1024]{1,0:T(2,128)S(1)} %get-tuple-element.243, f32[2,1024]{1,0:T(2,128)S(1)} %get-tuple-element.244, f32[2,1024]{1,0:T(2,128)S(1)} %get-tuple-element.245, f32[2,1024]{1,0:T(2,128)S(1)} %get-tuple-element.246, ...), kind=kOutput, calls=%fused_computation.40.clone.1 | convolution fusion | flops 1684013056 | bytes 5103624 | tf_op jit(solution)/shard_map/while/body/eval_jaxpr/gik,kr->gir/dot_general | solution.py:124
  114.4 11.7 %custom-call.42 = f32[2,64,64]{2,1,0:T(8,128)S(1)} custom-call(f32[2,64,64]{2,1,0:T(8,128)S(1)} %fusion.99), custom_call_target="Cholesky" | custom-call | tf_op jit(solution)/shard_map/while/body/eval_jaxpr/jit(cholesky)/cholesky | solution.py:85
  126.4 10.0 %custom-call.43 = f32[2,1,64,64]{2,3,1,0:T(8,128)S(1)} custom-call(f32[2,1,64,64]{3,2,1,0:T(8,128)S(1)} %select_bitcast_fusion.3), custom_call_target="InvertDiagBlocksLowerTriangular" | custom-call | tf_op jit(solution)/shard_map/while/body/eval_jaxpr/triangular_solve | solution.py:87
  136.4 20.7 %fusion.97 = f32[2,64,1024]{2,1,0:T(8,128)S(1)} fusion(f32[2,1024,64]{1,2,0:T(8,128)S(1)} %fusion.96, f32[2,1024]{1,0:T(2,128)S(1)} %get-tuple-element.241, f32[2,1024]{1,0:T(2,128)S(1)} %get-tuple-element.243, f32[2,1024]{1,0:T(2,128)S(1)} %get-tuple-element.244, f32[2,1024]{1,0:T(2,128)S(1)} %get-tuple-element.245, ...), kind=kOutput, calls=%fused_computation.39.clone.1 | convolution fusion | flops 1684013056 | bytes 5365768 | tf_op jit(solution)/shard_map/while/body/eval_jaxpr/gik,gir->grk/dot_general | solution.py:126
  160.5 21.1 %fusion.96 = f32[2,1024,64]{1,2,0:T(8,128)S(1)} fusion(f32[2,1024]{1,0:T(2,128)S(1)} %get-tuple-element.241, f32[2,1024]{1,0:T(2,128)S(1)} %get-tuple-element.243, f32[2,1024]{1,0:T(2,128)S(1)} %get-tuple-element.244, f32[2,1024]{1,0:T(2,128)S(1)} %get-tuple-element.245, f32[2,1024]{1,0:T(2,128)S(1)} %get-tuple-element.246, ...), kind=kOutput, calls=%fused_computation.40.clone.1 | convolution fusion | flops 1684013056 | bytes 5103624 | tf_op jit(solution)/shard_map/while/body/eval_jaxpr/gik,kr->gir/dot_general | solution.py:124
  182.5 11.7 %custom-call.42 = f32[2,64,64]{2,1,0:T(8,128)S(1)} custom-call(f32[2,64,64]{2,1,0:T(8,128)S(1)} %fusion.99), custom_call_target="Cholesky" | custom-call | tf_op jit(solution)/shard_map/while/body/eval_jaxpr/jit(cholesky)/cholesky | solution.py:85
  194.5 10.0 %custom-call.43 = f32[2,1,64,64]{2,3,1,0:T(8,128)S(1)} custom-call(f32[2,1,64,64]{3,2,1,0:T(8,128)S(1)} %select_bitcast_fusion.3), custom_call_target="InvertDiagBlocksLowerTriangular" | custom-call | tf_op jit(solution)/shard_map/while/body/eval_jaxpr/triangular_solve | solution.py:87
  204.5 20.8 %fusion.97 = f32[2,64,1024]{2,1,0:T(8,128)S(1)} fusion(f32[2,1024,64]{1,2,0:T(8,128)S(1)} %fusion.96, f32[2,1024]{1,0:T(2,128)S(1)} %get-tuple-element.241, f32[2,1024]{1,0:T(2,128)S(1)} %get-tuple-element.243, f32[2,1024]{1,0:T(2,128)S(1)} %get-tuple-element.244, f32[2,1024]{1,0:T(2,128)S(1)} %get-tuple-element.245, ...), kind=kOutput, calls=%fused_computation.39.clone.1 | convolution fusion | flops 1684013056 | bytes 5365768 | tf_op jit(solution)/shard_map/while/body/eval_jaxpr/gik,gir->grk/dot_general | solution.py:126
  228.6 21.1 %fusion.96 = f32[2,1024,64]{1,2,0:T(8,128)S(1)} fusion(f32[2,1024]{1,0:T(2,128)S(1)} %get-tuple-element.241, f32[2,1024]{1,0:T(2,128)S(1)} %get-tuple-element.243, f32[2,1024]{1,0:T(2,128)S(1)} %get-tuple-element.244, f32[2,1024]{1,0:T(2,128)S(1)} %get-tuple-element.245, f32[2,1024]{1,0:T(2,128)S(1)} %get-tuple-element.246, ...), kind=kOutput, calls=%fused_computation.40.clone.1 | convolution fusion | flops 1684013056 | bytes 5103624 | tf_op jit(solution)/shard_map/while/body/eval_jaxpr/gik,kr->gir/dot_general | solution.py:124
  250.7 11.7 %custom-call.42 = f32[2,64,64]{2,1,0:T(8,128)S(1)} custom-call(f32[2,64,64]{2,1,0:T(8,128)S(1)} %fusion.99), custom_call_target="Cholesky" | custom-call | tf_op jit(solution)/shard_map/while/body/eval_jaxpr/jit(cholesky)/cholesky | solution.py:85
  262.7 10.2 %custom-call.43 = f32[2,1,64,64]{2,3,1,0:T(8,128)S(1)} custom-call(f32[2,1,64,64]{3,2,1,0:T(8,128)S(1)} %select_bitcast_fusion.3), custom_call_target="InvertDiagBlocksLowerTriangular" | custom-call | tf_op jit(solution)/shard_map/while/body/eval_jaxpr/triangular_solve | solution.py:87
  272.9 20.6 %fusion.97 = f32[2,64,1024]{2,1,0:T(8,128)S(1)} fusion(f32[2,1024,64]{1,2,0:T(8,128)S(1)} %fusion.96, f32[2,1024]{1,0:T(2,128)S(1)} %get-tuple-element.241, f32[2,1024]{1,0:T(2,128)S(1)} %get-tuple-element.243, f32[2,1024]{1,0:T(2,128)S(1)} %get-tuple-element.244, f32[2,1024]{1,0:T(2,128)S(1)} %get-tuple-element.245, ...), kind=kOutput, calls=%fused_computation.39.clone.1 | convolution fusion | flops 1684013056 | bytes 5365768 | tf_op jit(solution)/shard_map/while/body/eval_jaxpr/gik,gir->grk/dot_general | solution.py:126
  323.5 9.3 %fusion.41 = (f32[64,1,64,512]{3,2,1,0:T(8,128)}, f32[64,1,64,512]{3,2,1,0:T(8,128)S(1)}) fusion(f32[64,64,512]{2,1,0:T(8,128)} %gather_fusion.10, pred[64]{0:T(512)(128)(4,1)S(1)} %copy-done.3, f32[64,64,512]{2,1,0:T(8,128)} %gather_fusion.8), kind=kLoop, calls=%fused_computation.95 | loop fusion | flops 4194304 | bytes 33554496 | tf_op jit(solution)/shard_map/jit(_where)/select_n | solution.py:195
  332.8 102.9 %all_to_all.60 = f32[64,1,64,512]{3,2,1,0:T(8,128)} all-to-all(f32[64,1,64,512]{3,2,1,0:T(8,128)S(1)} %get-tuple-element.164), channel_id=1, replica_groups=mesh['rows'=2,'cols'=64] {'cols'}, dimensions={0} | all-to-all | bytes 16777216 | tf_op jit(solution)/shard_map/all_to_all | solution.py:199
  435.7 7.9 %all-to-all-start.7 = ((f32[64,1,64,512]{3,2,1,0:T(8,128)}), f32[64,1,64,512]{3,2,1,0:T(8,128)}, u32[]{:S(2)}, u32[]{:S(2)}) async-start(f32[64,1,64,512]{3,2,1,0:T(8,128)} %get-tuple-element.163), calls=%async_computation.7 | async-start | bytes 16777216 | tf_op jit(solution)/shard_map/all_to_all | solution.py:200
  443.6 7.0 %gather_fusion.9 = f32[48,64,512]{2,1,0:T(8,128)} fusion(f32[64,64,512]{2,1,0:T(8,128)} %bitcast.201, s32[1024]{0:T(1024)S(1)} %pad_clamp_fusion), kind=kCustom, calls=%fused_computation.9 | custom fusion | bytes 12583104 | tf_op jit(solution)/shard_map/gather | solution.py:203
  450.7 111.5 %all-to-all-done.7 = f32[64,1,64,512]{3,2,1,0:T(8,128)} async-done(((f32[64,1,64,512]{3,2,1,0:T(8,128)}), f32[64,1,64,512]{3,2,1,0:T(8,128)}, u32[]{:S(2)}, u32[]{:S(2)}) %all-to-all-start.7) | async-done | bytes 8388640 | tf_op jit(solution)/shard_map/all_to_all | solution.py:200
  562.2 7.1 %gather_fusion.11 = f32[48,64,512]{2,1,0:T(8,128)} fusion(f32[64,64,512]{2,1,0:T(8,128)} %bitcast.64, s32[1024]{0:T(1024)S(1)} %pad_clamp_fusion), kind=kCustom, calls=%fused_computation.11 | custom fusion | bytes 12583104 | tf_op jit(solution)/shard_map/gather | solution.py:204
  569.3 12.4 %broadcast_select_fusion = (f32[48,64,512]{2,1,0:T(8,128)}, f32[48,64,512]{2,1,0:T(8,128)}) fusion(f32[48,64,512]{2,1,0:T(8,128)} %gather_fusion.11, pred[48]{0:T(512)(128)(4,1)S(1)} %iota_compare_fusion.4, f32[48,64,512]{2,1,0:T(8,128)} %gather_fusion.9), kind=kLoop, calls=%fused_computation.99 | loop fusion | flops 3145728 | bytes 25165872 | tf_op jit(solution)/shard_map/jit(_where)/select_n | solution.py:206
  (142 shorter events, 71.5 us)
Async XLA Ops:
  0.6 35.2 %copy-start = (f32[48,8,512]{2,1,0:T(8,128)S(1)}, f32[48,8,512]{2,1,0:T(8,128)}, u32[]{:S(2)}) copy-start(f32[48,8,512]{2,1,0:T(8,128)} %param.8) | copy-start | bytes 2359300
  2.0 19.0 %all-to-all-start = ((s32[64,1,1]{2,1,0:T(1,128)}), s32[64,1,1]{2,1,0:T(1,128)S(1)}, u32[]{:S(2)}, u32[]{:S(2)}) async-start(s32[64,1,1]{2,1,0:T(1,128)} %broadcast_in_dim.145), calls=%async_computation | async-start | bytes 65536 | tf_op jit(solution)/shard_map/all_to_all | solution.py:24
  28.9 14.4 %all-to-all-start.1 = ((f32[64,1,3]{2,1,0:T(1,128)}), f32[64,1,3]{2,1,0:T(1,128)S(1)}, u32[]{:S(2)}, u32[]{:S(2)}) async-start(f32[64,1,3]{2,1,0:T(1,128)} %copy.45), calls=%async_computation.1 | async-start | bytes 65536 | tf_op jit(solution)/shard_map/all_to_all | solution.py:175
  36.5 54.5 %copy-start.4 = (f32[1024,64]{0,1:T(8,128)S(1)}, f32[1024,64]{0,1:T(8,128)}, u32[]{:S(2)}) copy-start(f32[1024,64]{0,1:T(8,128)} %param.13) | copy-start | bytes 786436
  66.1 20.0 %all-to-all-start.3 = ((f32[64,1,8,512]{3,2,1,0:T(8,128)}), f32[64,1,8,512]{3,2,1,0:T(8,128)S(1)}, u32[]{:S(2)}, u32[]{:S(2)}) async-start(f32[64,1,8,512]{3,2,1,0:T(8,128)} %get-tuple-element.166), calls=%async_computation.3 | async-start | bytes 2097152 | tf_op jit(solution)/shard_map/all_to_all | solution.py:174
  92.1 21.3 %copy-start.2 = (s32[1024,1024]{1,0:T(8,128)}, s32[1024,1024]{1,0:T(8,128)S(1)}, u32[]{:S(2)}) copy-start(s32[1024,1024]{1,0:T(8,128)S(1)} %iota_subtract_fusion.2) | copy-start | bytes 12582916 | tf_op jit(solution)/shard_map/while
  160.5 21.1 %copy-start.2 = (s32[1024,1024]{1,0:T(8,128)}, s32[1024,1024]{1,0:T(8,128)S(1)}, u32[]{:S(2)}) copy-start(s32[1024,1024]{1,0:T(8,128)S(1)} %iota_subtract_fusion.2) | copy-start | bytes 12582916 | tf_op jit(solution)/shard_map/while
  228.6 21.2 %copy-start.2 = (s32[1024,1024]{1,0:T(8,128)}, s32[1024,1024]{1,0:T(8,128)S(1)}, u32[]{:S(2)}) copy-start(s32[1024,1024]{1,0:T(8,128)S(1)} %iota_subtract_fusion.2) | copy-start | bytes 12582916 | tf_op jit(solution)/shard_map/while
  318.9 4.6 copy-start.3
  435.7 126.5 %all-to-all-start.7 = ((f32[64,1,64,512]{3,2,1,0:T(8,128)}), f32[64,1,64,512]{3,2,1,0:T(8,128)}, u32[]{:S(2)}, u32[]{:S(2)}) async-start(f32[64,1,64,512]{3,2,1,0:T(8,128)} %get-tuple-element.163), calls=%async_computation.7 | async-start | bytes 16777216 | tf_op jit(solution)/shard_map/all_to_all | solution.py:200
  562.2 19.5 %copy-start.1 = (f32[48,8,512]{2,1,0:T(8,128)S(1)}, f32[48,8,512]{2,1,0:T(8,128)}, u32[]{:S(2)}) copy-start(f32[48,8,512]{2,1,0:T(8,128)} %param.8) | copy-start | bytes 2359300
